TPU v7x, 32 devices: a whole 2x2x4 slice. The times are simulated.
32 devices in a mesh: groups: 2 (over y), pool: 4 (over z), tensor: 2 (over x), sub: 2 (over core).
Axes of the slice: x: 2, y: 2, z: 4, core: 2. Of those that a mesh axis runs over, the one named last changes fastest.
Arguments:
- queries: bfloat16 [8, 160, 8192], P(('groups', 'pool'), None, ('tensor', 'sub')), parts along dimension 0, may hold values from -16 to 16
- new_keys: bfloat16 [8, 160, 1024], P(('groups', 'pool'), None, ('tensor', 'sub')), parts along dimension 0, may hold values from -9.6 to 9.6
- new_values: bfloat16 [8, 160, 1024], P(('groups', 'pool'), None, ('tensor', 'sub')), parts along dimension 0, may hold values from -6 to 6
- store_keys: bfloat16 [256, 256, 1024], P(('groups', 'pool'), None, ('tensor', 'sub')), parts along dimension 0, may hold values from -9.5625 to 9.5625
- store_values: bfloat16 [256, 256, 1024], P(('groups', 'pool'), None, ('tensor', 'sub')), parts along dimension 0, may hold values from -6 to 6
- prefix_blocks: int32 [8], P('groups'), parts along dimension 0, may hold values from 8 to 32, as said below
- hit_store: int32 [8, 32], P('groups'), parts along dimension 0, may hold values from 0 to 3, as said below
- hit_slot: int32 [8, 32], P('groups'), parts along dimension 0, may hold values from 0 to 31, as said below
- decode_owner: int32 [8], P('groups'), parts along dimension 0, may hold values from 0 to 3, as said below
Outputs:
- attended: bfloat16 [8, 160, 8192], P(('groups', 'pool'), None, ('tensor', 'sub')), parts along dimension 0
- pushed_keys: bfloat16 [16, 160, 1024], P(('groups', 'pool'), None, ('tensor', 'sub')), parts along dimension 0
- pushed_values: bfloat16 [16, 160, 1024], P(('groups', 'pool'), None, ('tensor', 'sub')), parts along dimension 0
There are 2 independent parts, one for each index of `groups`. A program takes and returns all parts, laid end to end along the dimension named above; each array names one. Nothing has to cross between parts.
Inputs may be any that keep to these rules, and one draw needn't show every extreme that they name: `prefix_blocks`: some request has exactly 32 cached blocks. `hit_store`: consecutive blocks of a request lie on store devices of consecutive index, wrapping around, so one store device holds at most 8 blocks of a request, and the request with 32 blocks puts exactly 8 on some store device. Entries past a request's count mean nothing. `hit_slot`: the cached blocks held by one store device occupy distinct slots. Entries past a request's count mean nothing. `decode_owner`: no instance decodes more than 2 requests, and some instance decodes exactly 2.
All inputs are finite; a program needn't handle non-finite values.
Results may differ from a plain program's by a relative error of at most 0.004.
Values may be sent and summed in bfloat16 or wider, within the bound.
No kernel may reach another device: no remote copies, remote signals or barrier semaphores. Data moves between devices by JAX's collectives and lax.ppermute only.
A program may use at most 128 MiB of HBM per device.

v0:
```python
import functools
import math

import jax
import jax.numpy as jnp
from jax import lax
from jax.experimental import pallas as pl
from jax.experimental.pallas import tpu as pltpu
from jax.sharding import PartitionSpec as P

HEADS = 64
KVH = 8
HD = 128
MAXBLK = 32
CAPP = 2
GROUP = HEADS // KVH
EMPTY = -1e30
TILE = 256
ONES = 16
PIECE = 32
SCALE = 1.0 / math.sqrt(HD)
EXP2_SCALE = SCALE * math.log2(math.e)
VMEM_LIMIT = 63 * 1024 * 1024 + 512 * 1024


def blocks_at(tables, request, place, pool_size):
    prefix_ref, store_ref, slot_ref = tables
    first = lax.rem(place - store_ref[request, 0] + pool_size, pool_size)
    count = lax.max(lax.div(prefix_ref[request] - first + pool_size - 1, pool_size), 0)
    return count, lambda entry: slot_ref[request, first + entry * pool_size]


def fetch(pool_size, tables, request, stores, buffers, sems, moved=None):
    me = lax.axis_index("pool")
    count, slot_of = blocks_at(tables, request, me if moved is None else me ^ 1, pool_size)

    def copies(entry):
        for i in range(2):
            if moved is None:
                source = stores[i].at[slot_of(entry)]
            else:
                source = moved.at[i * (moved.shape[0] // 2) + entry]
            yield pltpu.make_async_copy(source, buffers[i].at[entry], sems.at[i, entry])

    def start(entry, carry):
        for copy in copies(entry):
            copy.start()
        return carry

    lax.fori_loop(0, count, start, 0)

    def ready(entry):
        for copy in copies(entry):
            copy.wait()

    return count, ready


def gather_kernel(pool_size, prefix_ref, store_ref, slot_ref, store_keys, store_values, out_ref, sems):
    me = lax.axis_index("pool")
    capacity = out_ref.shape[0] // 2

    @pl.when(jnp.logical_not(is_inner(me)))
    def _():
        tables = (prefix_ref, store_ref, slot_ref)
        count, slot_of = blocks_at(tables, me ^ 3, me, pool_size)

        def copies(entry):
            return [
                pltpu.make_async_copy(
                    store.at[slot_of(entry)], out_ref.at[i * capacity + entry], sems.at[i, entry]
                )
                for i, store in enumerate((store_keys, store_values))
            ]

        def start(entry, carry):
            for copy in copies(entry):
                copy.start()
            return carry

        def wait(entry, carry):
            for copy in copies(entry):
                copy.wait()
            return carry

        lax.fori_loop(0, count, start, 0)
        lax.fori_loop(0, count, wait, 0)


def attend(
    key_ref,
    value_ref,
    count,
    ready,
    fresh,
    new_rows,
    columns,
    scores,
    weights,
    peaks,
    factors,
    turned,
    acc,
    initial=None,
    raw=False,
):
    rows = columns.shape[1]
    kv_local = columns.shape[0] // HD

    def visit(keys, values, seen):
        size = keys[0].shape[0]

        def score(kv):
            turned[kv, :HD, :size] = values[kv].T
            block = lax.dot_general(
                keys[kv],
                columns[kv * HD : (kv + 1) * HD, :],
                (((1,), (0,)), ((), ())),
                preferred_element_type=jnp.float32,
            )
            if seen is not None:
                block = jnp.where(seen, block, EMPTY)
            scores[kv, :size, :] = block

        def weigh(kv):
            for i in range(0, rows, TILE):
                part = slice(i, i + TILE)
                before = peaks[kv, :, part]
                block = scores[kv, :size, part]
                peak = jnp.maximum(before, jnp.max(block, axis=0, keepdims=True))
                factors[kv, :, part] = jnp.exp2((before - peak) * EXP2_SCALE)
                peaks[kv, :, part] = peak
                weight = jnp.exp2(block * EXP2_SCALE - peak[0:1] * EXP2_SCALE)
                weights[kv, :size, part] = weight.astype(jnp.bfloat16)

        def mix(kv):
            added = lax.dot_general(
                turned[kv, :, :size],
                weights[kv, :size, :],
                (((1,), (0,)), ((), ())),
                preferred_element_type=jnp.float32,
            )
            acc[kv] = acc[kv] * factors[kv, 0:1, :] + added

        for step in range(kv_local + 2):
            for offset, stage in ((0, score), (2, mix), (1, weigh)):
                if 0 <= step - offset < kv_local:
                    stage(step - offset)

    def lanes_of(array):
        return [array[:, kv * HD : (kv + 1) * HD] for kv in range(kv_local)]

    def blocks_of(ref, first, number):
        return lanes_of(ref[pl.ds(first, number)].reshape(number * ref.shape[1], ref.shape[2]))

    if initial is None:
        peaks[...] = jnp.full(peaks.shape, EMPTY, jnp.float32)
        acc[...] = jnp.zeros(acc.shape, jnp.float32)
    else:
        acc[...] = initial[0][...]
        peaks[...] = initial[1][...]
    turned[:, HD:, :] = jnp.ones((kv_local, ONES, turned.shape[2]), jnp.bfloat16)
    if fresh is not None:
        new_key_ref, new_value_ref = fresh
        row = lax.rem(lax.broadcasted_iota(jnp.int32, (1, rows), 1), new_rows)
        seen = lax.broadcasted_iota(jnp.int32, (new_key_ref.shape[0], rows), 0) <= row
        visit(lanes_of(new_key_ref), lanes_of(new_value_ref), seen)

    def visit_blocks(number):
        def body(index, carry):
            for i in range(number):
                ready(index * number + i)
            visit(
                blocks_of(key_ref, index * number, number),
                blocks_of(value_ref, index * number, number),
                None,
            )
            return carry

        return body

    pairs = count // 2 if key_ref.shape[0] > 1 else 0
    if key_ref.shape[0] > 1:
        lax.fori_loop(0, pairs, visit_blocks(2), 0)
    lax.fori_loop(2 * pairs, count, visit_blocks(1), 0)
    if raw:
        return acc[...], peaks[...]
    outs = []
    logs = []
    for kv in range(kv_local):
        total = acc[kv, HD : HD + 1, :]
        safe = jnp.where(total > 0, total, 1.0)
        logs.append(jnp.where(total > 0, peaks[kv, 0:1] * SCALE + jnp.log(safe), EMPTY))
        outs.append(acc[kv, :HD, :] * (1.0 / safe))
    return outs, logs


def prepare_kernel(query_ref, new_key_ref, new_value_ref, payload_ref, fresh_ref, query_rows):
    new_rows = query_ref.shape[0]
    kv_width = new_key_ref.shape[1]
    for kv in range(kv_width // HD):
        for g in range(GROUP):
            head = kv * GROUP + g
            query_rows[g * new_rows : (g + 1) * new_rows, :] = query_ref[
                :, head * HD : (head + 1) * HD
            ]
        payload_ref[kv * HD : (kv + 1) * HD, :] = query_rows[...].T
    for i, new_ref in enumerate((new_key_ref, new_value_ref)):
        for piece in range(new_rows // PIECE):
            row, lane = piece_place(i, piece, new_rows, kv_width)
            values = new_ref[piece * PIECE : (piece + 1) * PIECE, :]
            payload_ref[row : row + PIECE, lane : lane + kv_width] = values
            fresh_ref[row - kv_width : row - kv_width + PIECE, lane : lane + kv_width] = values


def piece_place(i, piece, new_rows, kv_width):
    index = i * (new_rows // PIECE) + piece
    beside = GROUP * new_rows // kv_width
    return kv_width + index // beside * PIECE, index % beside * kv_width


def payload_rows(new_rows, kv_width):
    return piece_place(1, new_rows // PIECE - 1, new_rows, kv_width)[0] + PIECE


def own_kernel(
    pool_size,
    prefix_ref,
    store_ref,
    slot_ref,
    payload_ref,
    new_key_ref,
    new_value_ref,
    store_keys,
    store_values,
    out_ref,
    log_ref,
    key_buf,
    value_buf,
    new_key_buf,
    new_value_buf,
    *state,
):
    *work, sems = state
    count, ready = fetch(
        pool_size,
        (prefix_ref, store_ref, slot_ref),
        lax.axis_index("pool"),
        (store_keys, store_values),
        (key_buf, value_buf),
        sems,
    )
    new_rows, kv_width = new_key_ref.shape
    for buffer, source in ((new_key_buf, new_key_ref), (new_value_buf, new_value_ref)):
        buffer[:new_rows, :] = source[...]
        buffer[new_rows:, :] = jnp.zeros((buffer.shape[0] - new_rows, kv_width), jnp.bfloat16)
    fresh = (new_key_buf, new_value_buf)
    outs, logs = attend(
        key_buf, value_buf, count, ready, fresh, new_rows, payload_ref.at[:kv_width], *work
    )
    log_ref[...] = jnp.zeros(log_ref.shape, jnp.float32)
    for kv, (out, log) in enumerate(zip(outs, logs)):
        out_ref[kv * HD : (kv + 1) * HD, :] = out
        log_ref[kv : kv + 1, :] = log


def other_kernel(pool_size, new_rows, partners, with_moved, raw, *refs):
    if partners is None:
        request = refs[0][0]
        choice = [None]
        refs = refs[1:]
    else:
        inner = is_inner(lax.axis_index("pool"))
        _, request = source_of(lax.axis_index("pool"), partners)
        choice = [
            hit for hit, mask in zip((inner, jnp.logical_not(inner)), partners) if mask is not None
        ]
    tables, refs = refs[:3], refs[3:]
    payload_refs, refs = refs[: len(choice)], refs[len(choice) :]
    moved = initial = None
    if with_moved:
        moved, *initial = refs[:3]
        refs = refs[3:]
    store_keys, store_values, *refs = refs
    out_refs, (key_buf, value_buf, *state) = refs[: 1 + raw], refs[1 + raw :]
    *work, columns, query_sem, sems = state
    kv_width = columns.shape[0]

    def query_copy(payload_ref):
        return pltpu.make_async_copy(payload_ref.at[:kv_width], columns, query_sem)

    def run():
        for payload_ref, hit in zip(payload_refs, choice):
            if len(choice) == 1:
                query_copy(payload_ref).start()
            else:
                pl.when(hit)(query_copy(payload_ref).start)
        count, ready = fetch(
            pool_size,
            tables,
            request,
            (store_keys, store_values),
            (key_buf, value_buf),
            sems,
            moved,
        )
        query_copy(payload_refs[0]).wait()
        results = attend(
            key_buf, value_buf, count, ready, None, new_rows, columns, *work, initial, raw
        )
        if raw:
            for out_ref, result in zip(out_refs, results):
                out_ref[...] = result
            return
        outs, logs = results
        out_ref = out_refs[0]
        tail = []
        for kv, (out, log) in enumerate(zip(outs, logs)):
            out_ref[kv * HD : (kv + 1) * HD, :] = out.astype(jnp.bfloat16)
            high = log.astype(jnp.bfloat16).astype(jnp.float32)
            middle = (log - high).astype(jnp.bfloat16).astype(jnp.float32)
            tail += [high, middle, log - high - middle]
        tail.append(jnp.zeros((ONES - len(tail), columns.shape[1]), jnp.float32))
        out_ref[kv_width:, :] = jnp.concatenate(tail, axis=0).astype(jnp.bfloat16)

    if len(choice) == 1 and choice[0] is not None:
        pl.when(choice[0])(run)
    else:
        run()


def is_inner(place):
    return (place == 1) | (place == 2)


def source_of(me, entry):
    if isinstance(entry, int):
        return jnp.bool_(True), jnp.int32(entry)
    inner = is_inner(me)
    masks = [0 if mask is None else mask for mask in entry]
    there = jnp.where(inner, entry[0] is not None, entry[1] is not None)
    return there, me ^ jnp.where(inner, masks[0], masks[1])


def push_kernel(pool_size, entries, owner_ref, *refs):
    payload_refs = refs[: len(entries)]
    key_out, value_out, sems = refs[len(entries) :]
    outs = (key_out, value_out)
    kv_width = key_out.shape[2]
    me = lax.axis_index("pool")
    total = jnp.int32(0)
    for other in range(pool_size):
        total += (owner_ref[other] == me).astype(jnp.int32)

    new_rows = key_out.shape[1]

    def copies(payload_ref, place):
        for i in range(2):
            for piece in range(new_rows // PIECE):
                row, lane = piece_place(i, piece, new_rows, kv_width)
                row += payload_ref.shape[0] - payload_rows(new_rows, kv_width)
                yield pltpu.make_async_copy(
                    payload_ref.at[row : row + PIECE, lane : lane + kv_width],
                    outs[i].at[place, piece * PIECE : (piece + 1) * PIECE],
                    sems.at[i, place, piece],
                )

    for entry, payload_ref in zip(entries, payload_refs):
        there, source = source_of(me, entry)
        rank = jnp.int32(0)
        for other in range(pool_size):
            rank += ((owner_ref[other] == me) & (other < source)).astype(jnp.int32)
        hit = there & (owner_ref[source] == me)
        for place in range(CAPP):

            @pl.when(hit & (rank == place))
            def _():
                for copy in copies(payload_ref, place):
                    copy.start()

    for place in range(CAPP):

        @pl.when(total <= place)
        def _():
            for out in outs:
                out[place] = jnp.zeros(out.shape[1:], jnp.bfloat16)

        @pl.when(total > place)
        def _():
            for copy in copies(payload_refs[0], place):
                copy.wait()


def combine_kernel(sources, last, own_ref, log_ref, *refs):
    parts = refs[: len(sources)]
    out_ref = refs[len(sources)]
    kv_width, rows = own_ref.shape
    me = lax.axis_index("pool")
    arrived = []
    tails = []
    for source, part in zip(sources, parts):
        there, request = source_of(me, source)
        arrived.append(there & (request != me))
        tails.append(part[kv_width:, :].astype(jnp.float32))
    if not last:
        refs[len(sources) + 1][...] = log_ref[...]
    for kv in range(kv_width // HD):
        logs = [log_ref[kv : kv + 1, :]]
        for there, tail in zip(arrived, tails):
            log = sum(tail[3 * kv + i : 3 * kv + i + 1] for i in range(3))
            logs.append(jnp.where(there, log, EMPTY))
        peak = functools.reduce(jnp.maximum, logs)
        shares = [jnp.exp(x - peak) for x in logs]
        total = functools.reduce(jnp.add, shares)
        shares = [x * (1.0 / total) for x in shares]
        band = slice(kv * HD, (kv + 1) * HD)
        for i in range(0, rows, TILE):
            part = slice(i, i + TILE)
            mixed = own_ref[band, part] * shares[0][:, part]
            for share, ref in zip(shares[1:], parts):
                mixed = mixed + ref[band, part].astype(jnp.float32) * share[:, part]
            if last:
                refs[len(sources) + 1][part, :] = mixed.astype(jnp.bfloat16).T
            else:
                out_ref[band, part] = mixed
        if last:
            turned = refs[len(sources) + 1]
            new_rows = out_ref.shape[0]
            for g in range(GROUP):
                head = kv * GROUP + g
                out_ref[:, head * HD : (head + 1) * HD] = turned[g * new_rows : (g + 1) * new_rows, :]
        else:
            refs[len(sources) + 1][kv : kv + 1, :] = peak + jnp.log(total)


def shards(
    queries,
    new_keys,
    new_values,
    store_keys,
    store_values,
    prefix_blocks,
    hit_store,
    hit_slot,
    decode_owner,
):
    pool_size = lax.axis_size("pool")
    capacity = (MAXBLK + pool_size - 1) // pool_size
    new_rows = queries.shape[1]
    width = queries.shape[2]
    kv_width = new_keys.shape[2]
    block_len = store_keys.shape[1]
    rows = GROUP * new_rows
    tables = (prefix_blocks, hit_store, hit_slot)
    smem_spec = pl.BlockSpec(memory_space=pltpu.SMEM)
    hbm_spec = pl.BlockSpec(memory_space=pltpu.HBM)
    vmem_spec = pl.BlockSpec(memory_space=pltpu.VMEM)
    params = pltpu.CompilerParams(vmem_limit_bytes=VMEM_LIMIT)

    def cost(share):
        return pl.CostEstimate(
            flops=share * rows * block_len * kv_width * capacity,
            bytes_accessed=rows,
            transcendentals=0,
        )

    buffers = [pltpu.VMEM((capacity, block_len, kv_width), jnp.bfloat16)] * 2
    kv_local = kv_width // HD
    widest = block_len * min(2, capacity)
    work = [
        pltpu.VMEM((kv_local, widest, rows), jnp.float32),
        pltpu.VMEM((kv_local, widest, rows), jnp.bfloat16),
        pltpu.VMEM((kv_local, 8, rows), jnp.float32),
        pltpu.VMEM((kv_local, 8, rows), jnp.float32),
        pltpu.VMEM((kv_local, HD + ONES, widest), jnp.bfloat16),
        pltpu.VMEM((kv_local, HD + ONES, rows), jnp.float32),
    ]
    sems = pltpu.SemaphoreType.DMA((2, capacity))

    def own_part(payload):
        return pl.pallas_call(
            functools.partial(own_kernel, pool_size),
            in_specs=[smem_spec] * 3 + [vmem_spec] * 3 + [hbm_spec] * 2,
            out_specs=[vmem_spec] * 2,
            scratch_shapes=[
                *buffers,
                *[pltpu.VMEM((block_len, kv_width), jnp.bfloat16)] * 2,
                *work,
                sems,
            ],
            out_shape=[
                jax.ShapeDtypeStruct((kv_width, rows), jnp.float32),
                jax.ShapeDtypeStruct((8, rows), jnp.float32),
            ],
            compiler_params=params,
            cost_estimate=cost(8),
            name="own_part",
        )(*tables, payload, new_keys[0], new_values[0], store_keys, store_values)

    def other_part(partners, held, *request, share=8, moved=(), raw=False):
        if raw:
            out_shape = [
                jax.ShapeDtypeStruct((kv_local, HD + ONES, rows), jnp.float32),
                jax.ShapeDtypeStruct((kv_local, 8, rows), jnp.float32),
            ]
        else:
            out_shape = jax.ShapeDtypeStruct((kv_width + ONES, rows), jnp.bfloat16)
        more_specs = [hbm_spec, vmem_spec, vmem_spec] if moved else []
        return pl.pallas_call(
            functools.partial(other_kernel, pool_size, new_rows, partners, bool(moved), raw),
            in_specs=[smem_spec] * (3 + len(request))
            + [hbm_spec] * len(held)
            + more_specs
            + [hbm_spec] * 2,
            out_specs=[vmem_spec] * 2 if raw else vmem_spec,
            scratch_shapes=[
                *buffers,
                *work,
                pltpu.VMEM((kv_width, rows), jnp.bfloat16),
                pltpu.SemaphoreType.DMA,
                sems,
            ],
            out_shape=out_shape,
            compiler_params=params,
            cost_estimate=cost(share),
            name="other_part",
        )(*request, *tables, *held, *moved, store_keys, store_values)

    def combine(own, log, sources, parts, last=True):
        if last:
            out_shape = jax.ShapeDtypeStruct((new_rows, width), jnp.bfloat16)
        else:
            out_shape = [
                jax.ShapeDtypeStruct((kv_width, rows), jnp.float32),
                jax.ShapeDtypeStruct((8, rows), jnp.float32),
            ]
        return pl.pallas_call(
            functools.partial(combine_kernel, tuple(sources), last),
            in_specs=[vmem_spec] * (2 + len(parts)),
            out_specs=vmem_spec if last else [vmem_spec] * 2,
            scratch_shapes=[pltpu.VMEM((rows, HD), jnp.bfloat16)] if last else [],
            out_shape=out_shape,
            compiler_params=params,
            cost_estimate=cost(0),
            name="combine",
        )(own, log, *parts)

    all_rows = payload_rows(new_rows, kv_width)
    payload, fresh = pl.pallas_call(
        prepare_kernel,
        in_specs=[vmem_spec] * 3,
        out_specs=[vmem_spec] * 2,
        scratch_shapes=[pltpu.VMEM((rows, HD), jnp.bfloat16)],
        out_shape=[
            jax.ShapeDtypeStruct((all_rows, rows), jnp.bfloat16),
            jax.ShapeDtypeStruct((all_rows - kv_width, rows), jnp.bfloat16),
        ],
        compiler_params=params,
        name="prepare",
    )(queries[0], new_keys[0], new_values[0])
    own_out, own_log = own_part(payload)
    if pool_size == 4:
        def send(array, *pairs):
            return lax.ppermute(array, "pool", pairs)

        near = send(payload, (0, 1), (1, 0), (2, 3), (3, 2))
        middle = send(payload, (1, 2), (2, 1))
        blocks = pl.pallas_call(
            functools.partial(gather_kernel, pool_size),
            in_specs=[smem_spec] * 3 + [hbm_spec] * 2,
            out_specs=vmem_spec,
            scratch_shapes=[sems],
            out_shape=jax.ShapeDtypeStruct((2 * capacity, block_len, kv_width), jnp.bfloat16),
            compiler_params=params,
            name="gather_blocks",
        )(*tables, store_keys, store_values)
        blocks = send(blocks, (0, 1), (3, 2))
        near, middle, own_out, own_log = lax.optimization_barrier((near, middle, own_out, own_log))
        crossed = send(near, (1, 2), (2, 1))
        outward = send(middle, (1, 0), (2, 3))
        first = other_part((3, 1), (middle, near))
        across = send(first, (1, 2), (2, 1))
        near, outward, first = lax.optimization_barrier((near, outward, first))
        second = other_part((1, 2), (near, outward), share=0)
        back = send(second, (1, 0), (2, 3))
        apart = send(second, (0, 2), (3, 1))
        first, crossed, second, fresh = lax.optimization_barrier((first, crossed, second, fresh))
        state = other_part((2, None), (crossed,), raw=True)
        inward = send(first, (0, 1), (3, 2))
        far = send(fresh, (0, 3), (3, 0))
        crossed, state = lax.optimization_barrier((crossed, state))
        third = other_part((2, None), (crossed,), moved=(blocks, *state))
        ends = send(third, (1, 3), (2, 0))
        own_out, own_log, third = lax.optimization_barrier((own_out, own_log, third))
        own_out, own_log = combine(
            own_out,
            own_log,
            [(3, None), (1, None), (2, None), (None, 1)],
            [across, inward, apart, back],
            last=False,
        )
        sources = [(None, 2)]
        parts = [ends]
        moved = [
            ((0, 0), payload),
            ((1, 1), near),
            ((3, None), middle),
            ((2, None), crossed),
            ((None, 2), outward),
            ((None, 3), far),
        ]
    else:
        gathered = lax.all_gather(payload, "pool", axis=0, tiled=False)
        packed = lax.map(
            lambda pair: other_part(None, (pair[0],), pair[1].reshape(1)),
            (gathered, jnp.arange(pool_size, dtype=jnp.int32)),
        )
        parts = lax.all_to_all(packed, "pool", split_axis=0, concat_axis=0, tiled=True)
        sources = list(range(pool_size))
        moved = [(source, gathered[source]) for source in range(pool_size)]

    attended = combine(own_out, own_log, sources, parts)
    pushed_keys, pushed_values = pl.pallas_call(
        functools.partial(push_kernel, pool_size, tuple(entry for entry, _ in moved)),
        in_specs=[smem_spec] + [hbm_spec] * len(moved),
        out_specs=[vmem_spec] * 2,
        scratch_shapes=[pltpu.SemaphoreType.DMA((2, CAPP, new_rows // PIECE))],
        out_shape=[jax.ShapeDtypeStruct((CAPP, new_rows, kv_width), jnp.bfloat16)] * 2,
        compiler_params=params,
        name="push",
    )(decode_owner, *[array for _, array in moved])
    return (attended[None], pushed_keys, pushed_values)


def solution(mesh):
    in_specs = (
        P(("groups", "pool"), None, ("tensor", "sub")),
        P(("groups", "pool"), None, ("tensor", "sub")),
        P(("groups", "pool"), None, ("tensor", "sub")),
        P(("groups", "pool"), None, ("tensor", "sub")),
        P(("groups", "pool"), None, ("tensor", "sub")),
        P("groups"),
        P("groups", None),
        P("groups", None),
        P("groups"),
    )
    out_specs = (
        P(("groups", "pool"), None, ("tensor", "sub")),
        P(("groups", "pool"), None, ("tensor", "sub")),
        P(("groups", "pool"), None, ("tensor", "sub")),
    )
    return jax.shard_map(shards, mesh=mesh, in_specs=in_specs, out_specs=out_specs, check_vma=False)
```

profile of v0, /device:TPU:0, one launch (start us, length us, event | category | flops | bytes accessed | tf_op | source)
XLA Modules:
  0.0 112.4 jit_solution(930352803038447129)
XLA Ops:
  0.6 2.3 %prepare.1 = (bf16[320,1280]{1,0:T(8,128)(2,1)}, bf16[64,1280]{1,0:T(8,128)(2,1)}) custom-call(bf16[160,2048]{1,0:T(8,128)(2,1)} %bitcast.4, bf16[160,256]{1,0:T(8,128)(2,1)} %bitcast.6, bf16[160,256]{1,0:T(8,128)(2,1)} %bitcast.8), custom_call_target="tpu_custom_call" | custom-call | tf_op jit(solution)/shard_map/prepare/pallas_call | solution.py:549
  3.0 3.0 %collective-permute-start = (bf16[320,1280]{1,0:T(8,128)(2,1)}, bf16[320,1280]{1,0:T(8,128)(2,1)}, u32[]{:S(2)}, u32[]{:S(2)}) collective-permute-start(bf16[320,1280]{1,0:T(8,128)(2,1)} %get-tuple-element.28.payload_ref.refs_0_), channel_id=1, source_target_pairs={{0,4},{4,0},{8,12},{12,8},{1,5},{5,1},{9,13},{13,9},{2,6},{6,2},{1... | collective-permute-start | bytes 2457608 | tf_op jit(solution)/shard_map/ppermute | solution.py:564
  6.0 1.6 %collective-permute-start.1 = (bf16[320,1280]{1,0:T(8,128)(2,1)}, bf16[320,1280]{1,0:T(8,128)(2,1)}, u32[]{:S(2)}, u32[]{:S(2)}) collective-permute-start(bf16[320,1280]{1,0:T(8,128)(2,1)} %get-tuple-element.28.payload_ref.refs_0_), channel_id=1, source_target_pairs={{4,8},{8,4},{5,9},{9,5},{6,10},{10,6},{7,11},{11,7},{20,24},{24,20... | collective-permute-start | bytes 2457608 | tf_op jit(solution)/shard_map/ppermute | solution.py:564
  7.6 3.8 %gather_blocks.1 = bf16[16,256,256]{2,1,0:T(8,128)(2,1)} custom-call(s32[4]{0:T(128)} %refs_0_.7, s32[4,32]{1,0:T(4,128)} %refs_1_.7, s32[4,32]{1,0:T(4,128)} %refs_2_.7, bf16[32,256,256]{2,1,0:T(8,128)(2,1)} %refs_7_.1, bf16[32,256,256]{2,1,0:T(8,128)(2,1)} %refs_8_.1), custom_call_target="tpu_custom_call" | custom-call | tf_op jit(solution)/shard_map/gather_blocks/pallas_call | solution.py:568
  11.5 5.1 %collective-permute-start.4 = (bf16[16,256,256]{2,1,0:T(8,128)(2,1)}, bf16[16,256,256]{2,1,0:T(8,128)(2,1)}, u32[]{:S(2)}, u32[]{:S(2)}) collective-permute-start(bf16[16,256,256]{2,1,0:T(8,128)(2,1)} %gather_blocks.1), channel_id=1, source_target_pairs={{0,4},{12,8},{1,5},{13,9},{2,6},{14,10},{3,7},{15,11},{16,20},{28,... | collective-permute-start | bytes 6291464 | tf_op jit(solution)/shard_map/ppermute | solution.py:564
  16.5 6.1 %own_part.1 = (f32[256,1280]{1,0:T(8,128)}, f32[8,1280]{1,0:T(8,128)}) custom-call(s32[4]{0:T(128)} %refs_0_.7, s32[4,32]{1,0:T(4,128)} %refs_1_.7, s32[4,32]{1,0:T(4,128)} %refs_2_.7, bf16[320,1280]{1,0:T(8,128)(2,1)} %get-tuple-element.28.payload_ref.refs_0_, bf16[160,256]{1,0:T(8,128)(2,1)} %bitcast.7, bf16[160,256]{1,0:T(8,128)(2,1)} %bitcast.9, ...), custom_call_target="tpu_custom_call" | custom-call | flops 5368709120 | bytes 1280 | tf_op jit(solution)/shard_map/own_part/pallas_call | solution.py:481
  22.7 2.3 %collective-permute-done.refs_4_.refs_3_.refs_1_ = bf16[320,1280]{1,0:T(8,128)(2,1)} collective-permute-done((bf16[320,1280]{1,0:T(8,128)(2,1)}, bf16[320,1280]{1,0:T(8,128)(2,1)}, u32[]{:S(2)}, u32[]{:S(2)}) %collective-permute-start) | collective-permute-done | bytes 819232 | tf_op jit(solution)/shard_map/ppermute | solution.py:564
  25.0 0.0 collective-permute-done.1.refs_3_.refs_2_
  25.0 1.3 %collective-permute-start.2 = (bf16[320,1280]{1,0:T(8,128)(2,1)}, bf16[320,1280]{1,0:T(8,128)(2,1)}, u32[]{:S(2)}, u32[]{:S(2)}) collective-permute-start(bf16[320,1280]{1,0:T(8,128)(2,1)} %collective-permute-done.1.refs_3_.refs_2_), channel_id=1, source_target_pairs={{4,0},{8,12},{5,1},{9,13},{6,2},{10,14},{7,3},{11,15},{20,16},{24,... | collective-permute-start | bytes 2457608 | tf_op jit(solution)/shard_map/ppermute | solution.py:564
  26.3 1.6 %collective-permute-start.3 = (bf16[320,1280]{1,0:T(8,128)(2,1)}, bf16[320,1280]{1,0:T(8,128)(2,1)}, u32[]{:S(2)}, u32[]{:S(2)}) collective-permute-start(bf16[320,1280]{1,0:T(8,128)(2,1)} %collective-permute-done.refs_4_.refs_3_.refs_1_), channel_id=1, source_target_pairs={{4,8},{8,4},{5,9},{9,5},{6,10},{10,6},{7,11},{11,7},{20,24},{24,20... | collective-permute-start | bytes 2457608 | tf_op jit(solution)/shard_map/ppermute | solution.py:564
  27.8 7.4 %other_part.4 = bf16[272,1280]{1,0:T(8,128)(2,1)} custom-call(s32[4]{0:T(128)} %refs_0_.7, s32[4,32]{1,0:T(4,128)} %refs_1_.7, s32[4,32]{1,0:T(4,128)} %refs_2_.7, bf16[320,1280]{1,0:T(8,128)(2,1)} %collective-permute-done.1.refs_3_.refs_2_, bf16[320,1280]{1,0:T(8,128)(2,1)} %collective-permute-done.refs_4_.refs_3_.refs_1_, bf16[32,256,256]{2,1,0:T(8,128)(2,1)} %refs_7_.1, ...), custom_call_target="tpu_custom_call" | custom-call | flops 5368709120 | bytes 1280 | tf_op jit(solution)/shard_map/other_part/pallas_call | solution.py:509
  35.2 1.5 %collective-permute-start.5 = (bf16[272,1280]{1,0:T(8,128)(2,1)}, bf16[272,1280]{1,0:T(8,128)(2,1)}, u32[]{:S(2)}, u32[]{:S(2)}) collective-permute-start(bf16[272,1280]{1,0:T(8,128)(2,1)} %other_part.4), channel_id=1, source_target_pairs={{4,8},{8,4},{5,9},{9,5},{6,10},{10,6},{7,11},{11,7},{20,24},{24,20... | collective-permute-start | bytes 2088968 | tf_op jit(solution)/shard_map/ppermute | solution.py:564
  36.7 11.6 %collective-permute-done.2.refs_4_ = bf16[320,1280]{1,0:T(8,128)(2,1)} collective-permute-done((bf16[320,1280]{1,0:T(8,128)(2,1)}, bf16[320,1280]{1,0:T(8,128)(2,1)}, u32[]{:S(2)}, u32[]{:S(2)}) %collective-permute-start.2) | collective-permute-done | bytes 819232 | tf_op jit(solution)/shard_map/ppermute | solution.py:564
  48.3 6.4 %other_part.5 = bf16[272,1280]{1,0:T(8,128)(2,1)} custom-call(s32[4]{0:T(128)} %refs_0_.7, s32[4,32]{1,0:T(4,128)} %refs_1_.7, s32[4,32]{1,0:T(4,128)} %refs_2_.7, bf16[320,1280]{1,0:T(8,128)(2,1)} %collective-permute-done.refs_4_.refs_3_.refs_1_, bf16[320,1280]{1,0:T(8,128)(2,1)} %collective-permute-done.2.refs_4_, bf16[32,256,256]{2,1,0:T(8,128)(2,1)} %refs_7_.1, ...), custom_call_target="tpu_custom_call" | custom-call | bytes 1280 | tf_op jit(solution)/shard_map/other_part/pallas_call | solution.py:509
  54.7 9.6 %collective-permute-start.7 = (bf16[272,1280]{1,0:T(8,128)(2,1)}, bf16[272,1280]{1,0:T(8,128)(2,1)}, u32[]{:S(2)}, u32[]{:S(2)}) collective-permute-start(bf16[272,1280]{1,0:T(8,128)(2,1)} %other_part.5), channel_id=1, source_target_pairs={{0,8},{12,4},{1,9},{13,5},{2,10},{14,6},{3,11},{15,7},{16,24},{28,... | collective-permute-start | bytes 2088968 | tf_op jit(solution)/shard_map/ppermute | solution.py:564
  64.3 1.3 %collective-permute-start.8 = (bf16[272,1280]{1,0:T(8,128)(2,1)}, bf16[272,1280]{1,0:T(8,128)(2,1)}, u32[]{:S(2)}, u32[]{:S(2)}) collective-permute-start(bf16[272,1280]{1,0:T(8,128)(2,1)} %other_part.5), channel_id=1, source_target_pairs={{4,0},{8,12},{5,1},{9,13},{6,2},{10,14},{7,3},{11,15},{20,16},{24,... | collective-permute-start | bytes 2088968 | tf_op jit(solution)/shard_map/ppermute | solution.py:564
  65.6 0.0 collective-permute-done.3.refs_3_
  65.6 0.0 copy-start.1
  65.6 2.4 %other_part.6 = (f32[2,144,1280]{2,1,0:T(8,128)}, f32[2,8,1280]{2,1,0:T(8,128)}) custom-call(s32[4]{0:T(128)} %refs_0_.7, s32[4,32]{1,0:T(4,128)} %refs_1_.7, s32[4,32]{1,0:T(4,128)} %refs_2_.7, bf16[320,1280]{1,0:T(8,128)(2,1)} %collective-permute-done.3.refs_3_, bf16[32,256,256]{2,1,0:T(8,128)(2,1)} %refs_7_.1, bf16[32,256,256]{2,1,0:T(8,128)(2,1)} %refs_8_.1), custom_call_target="tpu_custom_call" | custom-call | flops 5368709120 | bytes 1280 | tf_op jit(solution)/shard_map/other_part/pallas_call | solution.py:509
  68.0 1.9 %collective-permute-start.10 = (bf16[64,1280]{1,0:T(8,128)(2,1)S(1)}, bf16[64,1280]{1,0:T(8,128)(2,1)S(1)}, u32[]{:S(2)}, u32[]{:S(2)}) collective-permute-start(bf16[64,1280]{1,0:T(8,128)(2,1)S(1)} %copy-done.1), channel_id=1, source_target_pairs={{0,12},{12,0},{1,13},{13,1},{2,14},{14,2},{3,15},{15,3},{16,28},{2... | collective-permute-start | bytes 491528 | tf_op jit(solution)/shard_map/ppermute | solution.py:564
  69.9 0.0 collective-permute-done.4.refs_4_
  69.9 15.0 %collective-permute-start.6 = (bf16[272,1280]{1,0:T(8,128)(2,1)}, bf16[272,1280]{1,0:T(8,128)(2,1)}, u32[]{:S(2)}, u32[]{:S(2)}) collective-permute-start(bf16[272,1280]{1,0:T(8,128)(2,1)} %other_part.4), channel_id=1, source_target_pairs={{0,4},{12,8},{1,5},{13,9},{2,6},{14,10},{3,7},{15,11},{16,20},{28,... | collective-permute-start | bytes 2088968 | tf_op jit(solution)/shard_map/ppermute | solution.py:564
  84.9 2.4 %other_part.7 = bf16[272,1280]{1,0:T(8,128)(2,1)} custom-call(s32[4]{0:T(128)} %refs_0_.7, s32[4,32]{1,0:T(4,128)} %refs_1_.7, s32[4,32]{1,0:T(4,128)} %refs_2_.7, bf16[320,1280]{1,0:T(8,128)(2,1)} %collective-permute-done.3.refs_3_, bf16[16,256,256]{2,1,0:T(8,128)(2,1)} %collective-permute-done.4.refs_4_, f32[2,144,1280]{2,1,0:T(8,128)} %get-tuple-element.43.refs_5_, ...), custom_call_target="tpu_custom_call" | custom-call | flops 5368709120 | bytes 1280 | tf_op jit(solution)/shard_map/other_part/pallas_call | solution.py:509
  87.4 3.8 %collective-permute-done.10.refs_5_ = bf16[64,1280]{1,0:T(8,128)(2,1)S(1)} collective-permute-done((bf16[64,1280]{1,0:T(8,128)(2,1)S(1)}, bf16[64,1280]{1,0:T(8,128)(2,1)S(1)}, u32[]{:S(2)}, u32[]{:S(2)}) %collective-permute-start.10) | collective-permute-done | bytes 163872 | tf_op jit(solution)/shard_map/ppermute | solution.py:564
  91.2 1.3 %collective-permute-start.9 = (bf16[272,1280]{1,0:T(8,128)(2,1)}, bf16[272,1280]{1,0:T(8,128)(2,1)}, u32[]{:S(2)}, u32[]{:S(2)}) collective-permute-start(bf16[272,1280]{1,0:T(8,128)(2,1)} %other_part.7), channel_id=1, source_target_pairs={{4,12},{8,0},{5,13},{9,1},{6,14},{10,2},{7,15},{11,3},{20,28},{24,... | collective-permute-start | bytes 2088968 | tf_op jit(solution)/shard_map/ppermute | solution.py:564
  92.5 2.6 %push.1 = (bf16[2,160,256]{2,1,0:T(8,128)(2,1)}, bf16[2,160,256]{2,1,0:T(8,128)(2,1)}) custom-call(s32[4]{0:T(128)} %owner_ref.1, bf16[320,1280]{1,0:T(8,128)(2,1)} %get-tuple-element.28.payload_ref.refs_0_, bf16[320,1280]{1,0:T(8,128)(2,1)} %collective-permute-done.refs_4_.refs_3_.refs_1_, bf16[320,1280]{1,0:T(8,128)(2,1)} %collective-permute-done.1.refs_3_.refs_2_, ...), custom_call_target="tpu_custom_call" | custom-call | tf_op jit(solution)/shard_map/push/pallas_call | solution.py:623
  95.1 0.0 collective-permute-done.5.refs_0_
  95.1 7.0 %collective-permute-done.6.refs_1_ = bf16[272,1280]{1,0:T(8,128)(2,1)} collective-permute-done((bf16[272,1280]{1,0:T(8,128)(2,1)}, bf16[272,1280]{1,0:T(8,128)(2,1)}, u32[]{:S(2)}, u32[]{:S(2)}) %collective-permute-start.6) | collective-permute-done | bytes 696352 | tf_op jit(solution)/shard_map/ppermute | solution.py:564
  102.1 0.0 collective-permute-done.7.refs_2_
  102.1 4.0 %combine.2 = (f32[256,1280]{1,0:T(8,128)}, f32[8,1280]{1,0:T(8,128)}) custom-call(f32[256,1280]{1,0:T(8,128)} %get-tuple-element.45.own_ref, f32[8,1280]{1,0:T(8,128)} %get-tuple-element.46.log_ref, bf16[272,1280]{1,0:T(8,128)(2,1)} %collective-permute-done.5.refs_0_, bf16[272,1280]{1,0:T(8,128)(2,1)} %collective-permute-done.6.refs_1_, ...), custom_call_target="tpu_custom_call" | custom-call | bytes 1280 | tf_op jit(solution)/shard_map/combine/pallas_call | solution.py:537
  106.1 3.5 %collective-permute-done.9.refs_0_ = bf16[272,1280]{1,0:T(8,128)(2,1)} collective-permute-done((bf16[272,1280]{1,0:T(8,128)(2,1)}, bf16[272,1280]{1,0:T(8,128)(2,1)}, u32[]{:S(2)}, u32[]{:S(2)}) %collective-permute-start.9) | collective-permute-done | bytes 696352 | tf_op jit(solution)/shard_map/ppermute | solution.py:564
  109.6 2.8 %combine.3 = bf16[160,2048]{1,0:T(8,128)(2,1)} custom-call(f32[256,1280]{1,0:T(8,128)} %get-tuple-element.48.own_ref, f32[8,1280]{1,0:T(8,128)} %get-tuple-element.49.log_ref, bf16[272,1280]{1,0:T(8,128)(2,1)} %collective-permute-done.9.refs_0_), custom_call_target="tpu_custom_call" | custom-call | bytes 1280 | tf_op jit(solution)/shard_map/combine/pallas_call | solution.py:537
  (4 shorter events, 0.0 us)
Async XLA Ops:
  3.0 22.0 %collective-permute-start = (bf16[320,1280]{1,0:T(8,128)(2,1)}, bf16[320,1280]{1,0:T(8,128)(2,1)}, u32[]{:S(2)}, u32[]{:S(2)}) collective-permute-start(bf16[320,1280]{1,0:T(8,128)(2,1)} %get-tuple-element.28.payload_ref.refs_0_), channel_id=1, source_target_pairs={{0,4},{4,0},{8,12},{12,8},{1,5},{5,1},{9,13},{13,9},{2,6},{6,2},{1... | collective-permute-start | bytes 2457608 | tf_op jit(solution)/shard_map/ppermute | solution.py:564
  6.0 19.0 %collective-permute-start.1 = (bf16[320,1280]{1,0:T(8,128)(2,1)}, bf16[320,1280]{1,0:T(8,128)(2,1)}, u32[]{:S(2)}, u32[]{:S(2)}) collective-permute-start(bf16[320,1280]{1,0:T(8,128)(2,1)} %get-tuple-element.28.payload_ref.refs_0_), channel_id=1, source_target_pairs={{4,8},{8,4},{5,9},{9,5},{6,10},{10,6},{7,11},{11,7},{20,24},{24,20... | collective-permute-start | bytes 2457608 | tf_op jit(solution)/shard_map/ppermute | solution.py:564
  11.5 58.5 %collective-permute-start.4 = (bf16[16,256,256]{2,1,0:T(8,128)(2,1)}, bf16[16,256,256]{2,1,0:T(8,128)(2,1)}, u32[]{:S(2)}, u32[]{:S(2)}) collective-permute-start(bf16[16,256,256]{2,1,0:T(8,128)(2,1)} %gather_blocks.1), channel_id=1, source_target_pairs={{0,4},{12,8},{1,5},{13,9},{2,6},{14,10},{3,7},{15,11},{16,20},{28,... | collective-permute-start | bytes 6291464 | tf_op jit(solution)/shard_map/ppermute | solution.py:564
  25.0 23.3 %collective-permute-start.2 = (bf16[320,1280]{1,0:T(8,128)(2,1)}, bf16[320,1280]{1,0:T(8,128)(2,1)}, u32[]{:S(2)}, u32[]{:S(2)}) collective-permute-start(bf16[320,1280]{1,0:T(8,128)(2,1)} %collective-permute-done.1.refs_3_.refs_2_), channel_id=1, source_target_pairs={{4,0},{8,12},{5,1},{9,13},{6,2},{10,14},{7,3},{11,15},{20,16},{24,... | collective-permute-start | bytes 2457608 | tf_op jit(solution)/shard_map/ppermute | solution.py:564
  26.3 39.3 %collective-permute-start.3 = (bf16[320,1280]{1,0:T(8,128)(2,1)}, bf16[320,1280]{1,0:T(8,128)(2,1)}, u32[]{:S(2)}, u32[]{:S(2)}) collective-permute-start(bf16[320,1280]{1,0:T(8,128)(2,1)} %collective-permute-done.refs_4_.refs_3_.refs_1_), channel_id=1, source_target_pairs={{4,8},{8,4},{5,9},{9,5},{6,10},{10,6},{7,11},{11,7},{20,24},{24,20... | collective-permute-start | bytes 2457608 | tf_op jit(solution)/shard_map/ppermute | solution.py:564
  35.2 59.9 %collective-permute-start.5 = (bf16[272,1280]{1,0:T(8,128)(2,1)}, bf16[272,1280]{1,0:T(8,128)(2,1)}, u32[]{:S(2)}, u32[]{:S(2)}) collective-permute-start(bf16[272,1280]{1,0:T(8,128)(2,1)} %other_part.4), channel_id=1, source_target_pairs={{4,8},{8,4},{5,9},{9,5},{6,10},{10,6},{7,11},{11,7},{20,24},{24,20... | collective-permute-start | bytes 2088968 | tf_op jit(solution)/shard_map/ppermute | solution.py:564
  54.7 47.4 %collective-permute-start.7 = (bf16[272,1280]{1,0:T(8,128)(2,1)}, bf16[272,1280]{1,0:T(8,128)(2,1)}, u32[]{:S(2)}, u32[]{:S(2)}) collective-permute-start(bf16[272,1280]{1,0:T(8,128)(2,1)} %other_part.5), channel_id=1, source_target_pairs={{0,8},{12,4},{1,9},{13,5},{2,10},{14,6},{3,11},{15,7},{16,24},{28,... | collective-permute-start | bytes 2088968 | tf_op jit(solution)/shard_map/ppermute | solution.py:564
  64.3 37.8 %collective-permute-start.8 = (bf16[272,1280]{1,0:T(8,128)(2,1)}, bf16[272,1280]{1,0:T(8,128)(2,1)}, u32[]{:S(2)}, u32[]{:S(2)}) collective-permute-start(bf16[272,1280]{1,0:T(8,128)(2,1)} %other_part.5), channel_id=1, source_target_pairs={{4,0},{8,12},{5,1},{9,13},{6,2},{10,14},{7,3},{11,15},{20,16},{24,... | collective-permute-start | bytes 2088968 | tf_op jit(solution)/shard_map/ppermute | solution.py:564
  65.6 2.4 %copy-start.1 = (bf16[64,1280]{1,0:T(8,128)(2,1)S(1)}, bf16[64,1280]{1,0:T(8,128)(2,1)}, u32[]{:S(2)}) copy-start(bf16[64,1280]{1,0:T(8,128)(2,1)} %get-tuple-element.50) | copy-start | bytes 491524
  68.0 23.2 %collective-permute-start.10 = (bf16[64,1280]{1,0:T(8,128)(2,1)S(1)}, bf16[64,1280]{1,0:T(8,128)(2,1)S(1)}, u32[]{:S(2)}, u32[]{:S(2)}) collective-permute-start(bf16[64,1280]{1,0:T(8,128)(2,1)S(1)} %copy-done.1), channel_id=1, source_target_pairs={{0,12},{12,0},{1,13},{13,1},{2,14},{14,2},{3,15},{15,3},{16,28},{2... | collective-permute-start | bytes 491528 | tf_op jit(solution)/shard_map/ppermute | solution.py:564
  69.9 32.2 %collective-permute-start.6 = (bf16[272,1280]{1,0:T(8,128)(2,1)}, bf16[272,1280]{1,0:T(8,128)(2,1)}, u32[]{:S(2)}, u32[]{:S(2)}) collective-permute-start(bf16[272,1280]{1,0:T(8,128)(2,1)} %other_part.4), channel_id=1, source_target_pairs={{0,4},{12,8},{1,5},{13,9},{2,6},{14,10},{3,7},{15,11},{16,20},{28,... | collective-permute-start | bytes 2088968 | tf_op jit(solution)/shard_map/ppermute | solution.py:564
  91.2 1.3 %copy-start = (bf16[64,1280]{1,0:T(8,128)(2,1)}, bf16[64,1280]{1,0:T(8,128)(2,1)S(1)}, u32[]{:S(2)}) copy-start(bf16[64,1280]{1,0:T(8,128)(2,1)S(1)} %collective-permute-done.10.refs_5_) | copy-start | bytes 491524
  91.2 18.4 %collective-permute-start.9 = (bf16[272,1280]{1,0:T(8,128)(2,1)}, bf16[272,1280]{1,0:T(8,128)(2,1)}, u32[]{:S(2)}, u32[]{:S(2)}) collective-permute-start(bf16[272,1280]{1,0:T(8,128)(2,1)} %other_part.7), channel_id=1, source_target_pairs={{4,12},{8,0},{5,13},{9,1},{6,14},{10,2},{7,15},{11,3},{20,28},{24,... | collective-permute-start | bytes 2088968 | tf_op jit(solution)/shard_map/ppermute | solution.py:564
where the time goes:
time: 114 us; the launch traced here: 112 us
  starting transfers between devices  43.2 us (38%)
  Pallas kernels  40.3 us (35%)
  waiting for transfers between devices  28.2 us (25%)
    ppermute x11, starting transfers between devices, send(): return lax.ppermute(array, 'pool', pairs)  43.2 us
    ppermute x11, waiting for transfers between devices, send(): return lax.ppermute(array, 'pool', pairs)  28.2 us
    pallas_call x4, Pallas kernels, other_part(): pl.pallas_call(functools.partial(other_kernel, pool_size, new_rows, partn...  18.6 us
    pallas_call x2, Pallas kernels, combine(): pl.pallas_call(functools.partial(combine_kernel, tuple(sources), last), i...  6.8 us
    pallas_call x1, Pallas kernels, own_part(): pl.pallas_call(functools.partial(own_kernel, pool_size), in_specs=[smem_s...  6.13 us
    pallas_call x1, Pallas kernels, shards(): pl.pallas_call(functools.partial(gather_kernel, pool_size), in_specs=[sme...  3.83 us
    pallas_call x1, Pallas kernels, shards(): pl.pallas_call(functools.partial(push_kernel, pool_size, tuple((entry for...  2.59 us
    pallas_call x1, Pallas kernels, shards(): pl.pallas_call(prepare_kernel, in_specs=[vmem_spec] * 3, out_specs=[vmem_...  2.34 us
  transfers between devices with their start and end apart: 11, of which 5 were waited for; matrix products, arithmetic and copies ran while one was open for 0% of the time, Pallas kernels for 31%

commit v1 on v0

--- a/solution.py
+++ b/solution.py
@@ -433,6 +433,29 @@
             refs[len(sources) + 1][kv : kv + 1, :] = peak + jnp.log(total)
 
 
+def final_kernel(own_ref, log_ref, *refs):
+    part_refs, (out_ref, buffer, turned, sems) = refs[:4], refs[4:]
+    inner = is_inner(lax.axis_index("pool"))
+
+    def copies(first):
+        return [
+            pltpu.make_async_copy(part_refs[first + i], buffer.at[i], sems.at[i]) for i in range(2)
+        ]
+
+    for hit, first in ((inner, 0), (jnp.logical_not(inner), 2)):
+
+        @pl.when(hit)
+        def _():
+            for copy in copies(first):
+                copy.start()
+
+    for copy in copies(0):
+        copy.wait()
+    combine_kernel(
+        [(1, 1), (2, 2)], True, own_ref, log_ref, buffer.at[0], buffer.at[1], out_ref, turned
+    )
+
+
 def shards(
     queries,
     new_keys,
@@ -546,6 +569,21 @@
         )(own, log, *parts)
 
     all_rows = payload_rows(new_rows, kv_width)
+    def final(own, log, parts):
+        return pl.pallas_call(
+            final_kernel,
+            in_specs=[vmem_spec] * 2 + [hbm_spec] * 4,
+            out_specs=vmem_spec,
+            scratch_shapes=[
+                pltpu.VMEM((2, kv_width + ONES, rows), jnp.bfloat16),
+                pltpu.VMEM((rows, HD), jnp.bfloat16),
+                pltpu.SemaphoreType.DMA((2,)),
+            ],
+            out_shape=jax.ShapeDtypeStruct((new_rows, width), jnp.bfloat16),
+            compiler_params=params,
+            name="final",
+        )(own, log, *parts)
+
     payload, fresh = pl.pallas_call(
         prepare_kernel,
         in_specs=[vmem_spec] * 3,
@@ -575,7 +613,10 @@
             name="gather_blocks",
         )(*tables, store_keys, store_values)
         blocks = send(blocks, (0, 1), (3, 2))
-        near, middle, own_out, own_log = lax.optimization_barrier((near, middle, own_out, own_log))
+        far = send(fresh, (0, 3), (3, 0))
+        near, middle, far, own_out, own_log = lax.optimization_barrier(
+            (near, middle, far, own_out, own_log)
+        )
         crossed = send(near, (1, 2), (2, 1))
         outward = send(middle, (1, 0), (2, 3))
         first = other_part((3, 1), (middle, near))
@@ -584,23 +625,15 @@
         second = other_part((1, 2), (near, outward), share=0)
         back = send(second, (1, 0), (2, 3))
         apart = send(second, (0, 2), (3, 1))
-        first, crossed, second, fresh = lax.optimization_barrier((first, crossed, second, fresh))
+        first, crossed, second = lax.optimization_barrier((first, crossed, second))
         state = other_part((2, None), (crossed,), raw=True)
         inward = send(first, (0, 1), (3, 2))
-        far = send(fresh, (0, 3), (3, 0))
         crossed, state = lax.optimization_barrier((crossed, state))
         third = other_part((2, None), (crossed,), moved=(blocks, *state))
         ends = send(third, (1, 3), (2, 0))
         own_out, own_log, third = lax.optimization_barrier((own_out, own_log, third))
-        own_out, own_log = combine(
-            own_out,
-            own_log,
-            [(3, None), (1, None), (2, None), (None, 1)],
-            [across, inward, apart, back],
-            last=False,
-        )
-        sources = [(None, 2)]
-        parts = [ends]
+        own_out, own_log = combine(own_out, own_log, [(3, None)], [across], last=False)
+        attended = final(own_out, own_log, (inward, apart, back, ends))
         moved = [
             ((0, 0), payload),
             ((1, 1), near),
@@ -616,10 +649,9 @@
             (gathered, jnp.arange(pool_size, dtype=jnp.int32)),
         )
         parts = lax.all_to_all(packed, "pool", split_axis=0, concat_axis=0, tiled=True)
-        sources = list(range(pool_size))
+        attended = combine(own_out, own_log, list(range(pool_size)), parts)
         moved = [(source, gathered[source]) for source in range(pool_size)]
 
-    attended = combine(own_out, own_log, sources, parts)
     pushed_keys, pushed_values = pl.pallas_call(
         functools.partial(push_kernel, pool_size, tuple(entry for entry, _ in moved)),
         in_specs=[smem_spec] + [hbm_spec] * len(moved),

time: 114 us -> 161 us (1.41)
  waiting for transfers between devices: 28.2 us -> 73.9 us
  Pallas kernels: 40.3 us -> 49.5 us
  starting transfers between devices: 43.2 us -> 34.1 us
    ppermute x11, waiting for transfers between devices: 28.2 us -> 73.9 us  [send(): return lax.ppermute(array, 'pool', pairs)]
    ppermute x11, starting transfers between devices: 43.2 us -> 34.1 us  [send(): return lax.ppermute(array, 'pool', pairs)]
    pallas_call x1, Pallas kernels: 6.13 us -> 11.7 us  [own_part(): pl.pallas_call(functools.partial(own_kernel, pool_size), in_specs=[smem_s...]
    pallas_call x0 -> x1, Pallas kernels: none -> 4.05 us  [final(): pl.pallas_call(final_kernel, in_specs=[vmem_spec] * 2 + [hbm_spec] * 4, o...]
    pallas_call x4, Pallas kernels: 18.6 us -> 22.5 us  [other_part(): pl.pallas_call(functools.partial(other_kernel, pool_size, new_rows, partn...]
    pallas_call x2 -> x1, Pallas kernels: 6.8 us -> 2.88 us  [combine(): pl.pallas_call(functools.partial(combine_kernel, tuple(sources), last), i...]
  transfers between devices with their start and end apart: 11 -> 11, of which waited for: 5 -> 4; matrix products, arithmetic and copies ran while one was open for 0% -> 0% of each run, Pallas kernels for 31% -> 27%
where the time goes in v1:
time: 161 us; the launch traced here: 158 us
  waiting for transfers between devices  73.9 us (46%)
  Pallas kernels  49.5 us (31%)
  starting transfers between devices  34.1 us (21%)
    ppermute x11, waiting for transfers between devices, send(): return lax.ppermute(array, 'pool', pairs)  73.9 us
    ppermute x11, starting transfers between devices, send(): return lax.ppermute(array, 'pool', pairs)  34.1 us
    pallas_call x4, Pallas kernels, other_part(): pl.pallas_call(functools.partial(other_kernel, pool_size, new_rows, partn...  22.5 us
    pallas_call x1, Pallas kernels, own_part(): pl.pallas_call(functools.partial(own_kernel, pool_size), in_specs=[smem_s...  11.7 us
    pallas_call x1, Pallas kernels, final(): pl.pallas_call(final_kernel, in_specs=[vmem_spec] * 2 + [hbm_spec] * 4, o...  4.05 us
    pallas_call x1, Pallas kernels, shards(): pl.pallas_call(functools.partial(gather_kernel, pool_size), in_specs=[sme...  3.51 us
  transfers between devices with their start and end apart: 11, of which 4 were waited for; matrix products, arithmetic and copies ran while one was open for 0% of the time, Pallas kernels for 27%

profile of v1, /device:TPU:0, one launch (start us, length us, event | category | flops | bytes accessed | tf_op | source)
XLA Modules:
  0.0 158.4 jit_solution(581899248267106295)
XLA Ops:
  0.6 2.3 %prepare.1 = (bf16[320,1280]{1,0:T(8,128)(2,1)}, bf16[64,1280]{1,0:T(8,128)(2,1)}) custom-call(bf16[160,2048]{1,0:T(8,128)(2,1)} %bitcast.5, bf16[160,256]{1,0:T(8,128)(2,1)} %bitcast.6, bf16[160,256]{1,0:T(8,128)(2,1)} %bitcast.8), custom_call_target="tpu_custom_call" | custom-call | tf_op jit(solution)/shard_map/prepare/pallas_call | solution.py:587
  3.0 3.0 %collective-permute-start = (bf16[320,1280]{1,0:T(8,128)(2,1)}, bf16[320,1280]{1,0:T(8,128)(2,1)}, u32[]{:S(2)}, u32[]{:S(2)}) collective-permute-start(bf16[320,1280]{1,0:T(8,128)(2,1)} %get-tuple-element.28.payload_ref.refs_0_), channel_id=1, source_target_pairs={{0,4},{4,0},{8,12},{12,8},{1,5},{5,1},{9,13},{13,9},{2,6},{6,2},{1... | collective-permute-start | bytes 2457608 | tf_op jit(solution)/shard_map/ppermute | solution.py:602
  6.0 1.6 %collective-permute-start.1 = (bf16[320,1280]{1,0:T(8,128)(2,1)}, bf16[320,1280]{1,0:T(8,128)(2,1)}, u32[]{:S(2)}, u32[]{:S(2)}) collective-permute-start(bf16[320,1280]{1,0:T(8,128)(2,1)} %get-tuple-element.28.payload_ref.refs_0_), channel_id=1, source_target_pairs={{4,8},{8,4},{5,9},{9,5},{6,10},{10,6},{7,11},{11,7},{20,24},{24,20... | collective-permute-start | bytes 2457608 | tf_op jit(solution)/shard_map/ppermute | solution.py:602
  7.6 3.5 %gather_blocks.1 = bf16[16,256,256]{2,1,0:T(8,128)(2,1)} custom-call(s32[4]{0:T(128)} %refs_0_.7, s32[4,32]{1,0:T(4,128)} %refs_1_.7, s32[4,32]{1,0:T(4,128)} %refs_2_.7, bf16[32,256,256]{2,1,0:T(8,128)(2,1)} %refs_7_.1, bf16[32,256,256]{2,1,0:T(8,128)(2,1)} %refs_8_.1), custom_call_target="tpu_custom_call" | custom-call | tf_op jit(solution)/shard_map/gather_blocks/pallas_call | solution.py:606
  11.2 5.4 %collective-permute-start.5 = (bf16[16,256,256]{2,1,0:T(8,128)(2,1)}, bf16[16,256,256]{2,1,0:T(8,128)(2,1)}, u32[]{:S(2)}, u32[]{:S(2)}) collective-permute-start(bf16[16,256,256]{2,1,0:T(8,128)(2,1)} %gather_blocks.1), channel_id=1, source_target_pairs={{0,4},{12,8},{1,5},{13,9},{2,6},{14,10},{3,7},{15,11},{16,20},{28,... | collective-permute-start | bytes 6291464 | tf_op jit(solution)/shard_map/ppermute | solution.py:602
  16.5 2.8 %collective-permute-start.2 = (bf16[64,1280]{1,0:T(8,128)(2,1)S(1)}, bf16[64,1280]{1,0:T(8,128)(2,1)S(1)}, u32[]{:S(2)}, u32[]{:S(2)}) collective-permute-start(bf16[64,1280]{1,0:T(8,128)(2,1)S(1)} %copy-done.1), channel_id=1, source_target_pairs={{0,12},{12,0},{1,13},{13,1},{2,14},{14,2},{3,15},{15,3},{16,28},{2... | collective-permute-start | bytes 491528 | tf_op jit(solution)/shard_map/ppermute | solution.py:602
  19.4 11.7 %own_part.1 = (f32[256,1280]{1,0:T(8,128)}, f32[8,1280]{1,0:T(8,128)}) custom-call(s32[4]{0:T(128)} %refs_0_.7, s32[4,32]{1,0:T(4,128)} %refs_1_.7, s32[4,32]{1,0:T(4,128)} %refs_2_.7, bf16[320,1280]{1,0:T(8,128)(2,1)} %get-tuple-element.28.payload_ref.refs_0_, bf16[160,256]{1,0:T(8,128)(2,1)} %bitcast.7, bf16[160,256]{1,0:T(8,128)(2,1)} %bitcast.9, ...), custom_call_target="tpu_custom_call" | custom-call | flops 5368709120 | bytes 1280 | tf_op jit(solution)/shard_map/own_part/pallas_call | solution.py:504
  31.0 44.1 %collective-permute-done.2.refs_5_ = bf16[64,1280]{1,0:T(8,128)(2,1)S(1)} collective-permute-done((bf16[64,1280]{1,0:T(8,128)(2,1)S(1)}, bf16[64,1280]{1,0:T(8,128)(2,1)S(1)}, u32[]{:S(2)}, u32[]{:S(2)}) %collective-permute-start.2) | collective-permute-done | bytes 163872 | tf_op jit(solution)/shard_map/ppermute | solution.py:602
  75.1 0.0 collective-permute-done.refs_4_.refs_3_.refs_1_
  75.1 0.0 collective-permute-done.1.refs_3_.refs_2_
  75.1 1.3 collective-permute-start.3
  76.4 1.6 collective-permute-start.4
  78.0 6.4 %other_part.4 = bf16[272,1280]{1,0:T(8,128)(2,1)} custom-call(s32[4]{0:T(128)} %refs_0_.7, s32[4,32]{1,0:T(4,128)} %refs_1_.7, s32[4,32]{1,0:T(4,128)} %refs_2_.7, bf16[320,1280]{1,0:T(8,128)(2,1)} %collective-permute-done.1.refs_3_.refs_2_, bf16[320,1280]{1,0:T(8,128)(2,1)} %collective-permute-done.refs_4_.refs_3_.refs_1_, bf16[32,256,256]{2,1,0:T(8,128)(2,1)} %refs_7_.1, ...), custom_call_target="tpu_custom_call" | custom-call | flops 5368709120 | bytes 1280 | tf_op jit(solution)/shard_map/other_part/pallas_call | solution.py:532
  84.4 1.5 collective-permute-start.6
  85.9 10.5 %collective-permute-done.3.refs_4_ = bf16[320,1280]{1,0:T(8,128)(2,1)} collective-permute-done((bf16[320,1280]{1,0:T(8,128)(2,1)}, bf16[320,1280]{1,0:T(8,128)(2,1)}, u32[]{:S(2)}, u32[]{:S(2)}) %collective-permute-start.3) | collective-permute-done | bytes 819232 | tf_op jit(solution)/shard_map/ppermute | solution.py:602
  96.4 11.6 %other_part.5 = bf16[272,1280]{1,0:T(8,128)(2,1)} custom-call(s32[4]{0:T(128)} %refs_0_.7, s32[4,32]{1,0:T(4,128)} %refs_1_.7, s32[4,32]{1,0:T(4,128)} %refs_2_.7, bf16[320,1280]{1,0:T(8,128)(2,1)} %collective-permute-done.refs_4_.refs_3_.refs_1_, bf16[320,1280]{1,0:T(8,128)(2,1)} %collective-permute-done.3.refs_4_, bf16[32,256,256]{2,1,0:T(8,128)(2,1)} %refs_7_.1, ...), custom_call_target="tpu_custom_call" | custom-call | bytes 1280 | tf_op jit(solution)/shard_map/other_part/pallas_call | solution.py:532
  108.1 2.2 %collective-permute-start.8 = (bf16[272,1280]{1,0:T(8,128)(2,1)}, bf16[272,1280]{1,0:T(8,128)(2,1)}, u32[]{:S(2)}, u32[]{:S(2)}) collective-permute-start(bf16[272,1280]{1,0:T(8,128)(2,1)} %other_part.5), channel_id=1, source_target_pairs={{0,8},{12,4},{1,9},{13,5},{2,10},{14,6},{3,11},{15,7},{16,24},{28,... | collective-permute-start | bytes 2088968 | tf_op jit(solution)/shard_map/ppermute | solution.py:602
  110.2 1.5 collective-permute-start.9
  111.7 0.0 collective-permute-done.4.refs_3_
  111.7 2.0 %other_part.6 = (f32[2,144,1280]{2,1,0:T(8,128)}, f32[2,8,1280]{2,1,0:T(8,128)}) custom-call(s32[4]{0:T(128)} %refs_0_.7, s32[4,32]{1,0:T(4,128)} %refs_1_.7, s32[4,32]{1,0:T(4,128)} %refs_2_.7, bf16[320,1280]{1,0:T(8,128)(2,1)} %collective-permute-done.4.refs_3_, bf16[32,256,256]{2,1,0:T(8,128)(2,1)} %refs_7_.1, bf16[32,256,256]{2,1,0:T(8,128)(2,1)} %refs_8_.1), custom_call_target="tpu_custom_call" | custom-call | flops 5368709120 | bytes 1280 | tf_op jit(solution)/shard_map/other_part/pallas_call | solution.py:532
  113.8 11.9 %collective-permute-start.7 = (bf16[272,1280]{1,0:T(8,128)(2,1)}, bf16[272,1280]{1,0:T(8,128)(2,1)}, u32[]{:S(2)}, u32[]{:S(2)}) collective-permute-start(bf16[272,1280]{1,0:T(8,128)(2,1)} %other_part.4), channel_id=1, source_target_pairs={{0,4},{12,8},{1,5},{13,9},{2,6},{14,10},{3,7},{15,11},{16,20},{28,... | collective-permute-start | bytes 2088968 | tf_op jit(solution)/shard_map/ppermute | solution.py:602
  125.7 0.0 collective-permute-done.5.refs_4_
  125.7 2.4 %other_part.7 = bf16[272,1280]{1,0:T(8,128)(2,1)} custom-call(s32[4]{0:T(128)} %refs_0_.7, s32[4,32]{1,0:T(4,128)} %refs_1_.7, s32[4,32]{1,0:T(4,128)} %refs_2_.7, bf16[320,1280]{1,0:T(8,128)(2,1)} %collective-permute-done.4.refs_3_, bf16[16,256,256]{2,1,0:T(8,128)(2,1)} %collective-permute-done.5.refs_4_, f32[2,144,1280]{2,1,0:T(8,128)} %get-tuple-element.43.refs_5_, ...), custom_call_target="tpu_custom_call" | custom-call | flops 5368709120 | bytes 1280 | tf_op jit(solution)/shard_map/other_part/pallas_call | solution.py:532
  128.1 1.3 collective-permute-start.10
  129.4 2.6 %push.1 = (bf16[2,160,256]{2,1,0:T(8,128)(2,1)}, bf16[2,160,256]{2,1,0:T(8,128)(2,1)}) custom-call(s32[4]{0:T(128)} %owner_ref.1, bf16[320,1280]{1,0:T(8,128)(2,1)} %get-tuple-element.28.payload_ref.refs_0_, bf16[320,1280]{1,0:T(8,128)(2,1)} %collective-permute-done.refs_4_.refs_3_.refs_1_, bf16[320,1280]{1,0:T(8,128)(2,1)} %collective-permute-done.1.refs_3_.refs_2_, ...), custom_call_target="tpu_custom_call" | custom-call | tf_op jit(solution)/shard_map/push/pallas_call | solution.py:655
  132.0 0.0 collective-permute-done.6.refs_0_
  132.0 2.9 %combine.1 = (f32[256,1280]{1,0:T(8,128)}, f32[8,1280]{1,0:T(8,128)}) custom-call(f32[256,1280]{1,0:T(8,128)} %get-tuple-element.45.own_ref, f32[8,1280]{1,0:T(8,128)} %get-tuple-element.46.log_ref, bf16[272,1280]{1,0:T(8,128)(2,1)} %collective-permute-done.6.refs_0_), custom_call_target="tpu_custom_call" | custom-call | bytes 1280 | tf_op jit(solution)/shard_map/combine/pallas_call | solution.py:560
  134.9 3.1 %collective-permute-done.7.refs_0_ = bf16[272,1280]{1,0:T(8,128)(2,1)} collective-permute-done((bf16[272,1280]{1,0:T(8,128)(2,1)}, bf16[272,1280]{1,0:T(8,128)(2,1)}, u32[]{:S(2)}, u32[]{:S(2)}) %collective-permute-start.7) | collective-permute-done | bytes 696352 | tf_op jit(solution)/shard_map/ppermute | solution.py:602
  138.0 0.0 collective-permute-done.8.refs_1_
  138.0 0.0 collective-permute-done.9.refs_2_
  138.0 16.2 %collective-permute-done.10.refs_3_ = bf16[272,1280]{1,0:T(8,128)(2,1)} collective-permute-done((bf16[272,1280]{1,0:T(8,128)(2,1)}, bf16[272,1280]{1,0:T(8,128)(2,1)}, u32[]{:S(2)}, u32[]{:S(2)}) %collective-permute-start.10) | collective-permute-done | bytes 696352 | tf_op jit(solution)/shard_map/ppermute | solution.py:602
  154.2 4.1 %final.1 = bf16[160,2048]{1,0:T(8,128)(2,1)} custom-call(f32[256,1280]{1,0:T(8,128)} %get-tuple-element.47.own_ref, f32[8,1280]{1,0:T(8,128)} %get-tuple-element.48.log_ref, bf16[272,1280]{1,0:T(8,128)(2,1)} %collective-permute-done.7.refs_0_, bf16[272,1280]{1,0:T(8,128)(2,1)} %collective-permute-done.8.refs_1_, ...), custom_call_target="tpu_custom_call" | custom-call | tf_op jit(solution)/shard_map/final/pallas_call | solution.py:573
  (4 shorter events, 0.0 us)
Async XLA Ops:
  3.0 13.6 %copy-start.1 = (bf16[64,1280]{1,0:T(8,128)(2,1)S(1)}, bf16[64,1280]{1,0:T(8,128)(2,1)}, u32[]{:S(2)}) copy-start(bf16[64,1280]{1,0:T(8,128)(2,1)} %get-tuple-element.29) | copy-start | bytes 491524
  3.0 72.1 %collective-permute-start = (bf16[320,1280]{1,0:T(8,128)(2,1)}, bf16[320,1280]{1,0:T(8,128)(2,1)}, u32[]{:S(2)}, u32[]{:S(2)}) collective-permute-start(bf16[320,1280]{1,0:T(8,128)(2,1)} %get-tuple-element.28.payload_ref.refs_0_), channel_id=1, source_target_pairs={{0,4},{4,0},{8,12},{12,8},{1,5},{5,1},{9,13},{13,9},{2,6},{6,2},{1... | collective-permute-start | bytes 2457608 | tf_op jit(solution)/shard_map/ppermute | solution.py:602
  6.0 69.1 %collective-permute-start.1 = (bf16[320,1280]{1,0:T(8,128)(2,1)}, bf16[320,1280]{1,0:T(8,128)(2,1)}, u32[]{:S(2)}, u32[]{:S(2)}) collective-permute-start(bf16[320,1280]{1,0:T(8,128)(2,1)} %get-tuple-element.28.payload_ref.refs_0_), channel_id=1, source_target_pairs={{4,8},{8,4},{5,9},{9,5},{6,10},{10,6},{7,11},{11,7},{20,24},{24,20... | collective-permute-start | bytes 2457608 | tf_op jit(solution)/shard_map/ppermute | solution.py:602
  11.2 114.6 %collective-permute-start.5 = (bf16[16,256,256]{2,1,0:T(8,128)(2,1)}, bf16[16,256,256]{2,1,0:T(8,128)(2,1)}, u32[]{:S(2)}, u32[]{:S(2)}) collective-permute-start(bf16[16,256,256]{2,1,0:T(8,128)(2,1)} %gather_blocks.1), channel_id=1, source_target_pairs={{0,4},{12,8},{1,5},{13,9},{2,6},{14,10},{3,7},{15,11},{16,20},{28,... | collective-permute-start | bytes 6291464 | tf_op jit(solution)/shard_map/ppermute | solution.py:602
  16.5 58.6 %collective-permute-start.2 = (bf16[64,1280]{1,0:T(8,128)(2,1)S(1)}, bf16[64,1280]{1,0:T(8,128)(2,1)S(1)}, u32[]{:S(2)}, u32[]{:S(2)}) collective-permute-start(bf16[64,1280]{1,0:T(8,128)(2,1)S(1)} %copy-done.1), channel_id=1, source_target_pairs={{0,12},{12,0},{1,13},{13,1},{2,14},{14,2},{3,15},{15,3},{16,28},{2... | collective-permute-start | bytes 491528 | tf_op jit(solution)/shard_map/ppermute | solution.py:602
  75.1 9.3 %copy-start = (bf16[64,1280]{1,0:T(8,128)(2,1)}, bf16[64,1280]{1,0:T(8,128)(2,1)S(1)}, u32[]{:S(2)}) copy-start(bf16[64,1280]{1,0:T(8,128)(2,1)S(1)} %collective-permute-done.2.refs_5_) | copy-start | bytes 491524
  75.1 21.3 %collective-permute-start.3 = (bf16[320,1280]{1,0:T(8,128)(2,1)}, bf16[320,1280]{1,0:T(8,128)(2,1)}, u32[]{:S(2)}, u32[]{:S(2)}) collective-permute-start(bf16[320,1280]{1,0:T(8,128)(2,1)} %collective-permute-done.1.refs_3_.refs_2_), channel_id=1, source_target_pairs={{4,0},{8,12},{5,1},{9,13},{6,2},{10,14},{7,3},{11,15},{20,16},{24,... | collective-permute-start | bytes 2457608 | tf_op jit(solution)/shard_map/ppermute | solution.py:602
  76.4 35.3 %collective-permute-start.4 = (bf16[320,1280]{1,0:T(8,128)(2,1)}, bf16[320,1280]{1,0:T(8,128)(2,1)}, u32[]{:S(2)}, u32[]{:S(2)}) collective-permute-start(bf16[320,1280]{1,0:T(8,128)(2,1)} %collective-permute-done.refs_4_.refs_3_.refs_1_), channel_id=1, source_target_pairs={{4,8},{8,4},{5,9},{9,5},{6,10},{10,6},{7,11},{11,7},{20,24},{24,20... | collective-permute-start | bytes 2457608 | tf_op jit(solution)/shard_map/ppermute | solution.py:602
  84.4 47.6 %collective-permute-start.6 = (bf16[272,1280]{1,0:T(8,128)(2,1)}, bf16[272,1280]{1,0:T(8,128)(2,1)}, u32[]{:S(2)}, u32[]{:S(2)}) collective-permute-start(bf16[272,1280]{1,0:T(8,128)(2,1)} %other_part.4), channel_id=1, source_target_pairs={{4,8},{8,4},{5,9},{9,5},{6,10},{10,6},{7,11},{11,7},{20,24},{24,20... | collective-permute-start | bytes 2088968 | tf_op jit(solution)/shard_map/ppermute | solution.py:602
  108.1 29.9 %collective-permute-start.8 = (bf16[272,1280]{1,0:T(8,128)(2,1)}, bf16[272,1280]{1,0:T(8,128)(2,1)}, u32[]{:S(2)}, u32[]{:S(2)}) collective-permute-start(bf16[272,1280]{1,0:T(8,128)(2,1)} %other_part.5), channel_id=1, source_target_pairs={{0,8},{12,4},{1,9},{13,5},{2,10},{14,6},{3,11},{15,7},{16,24},{28,... | collective-permute-start | bytes 2088968 | tf_op jit(solution)/shard_map/ppermute | solution.py:602
  110.2 27.8 %collective-permute-start.9 = (bf16[272,1280]{1,0:T(8,128)(2,1)}, bf16[272,1280]{1,0:T(8,128)(2,1)}, u32[]{:S(2)}, u32[]{:S(2)}) collective-permute-start(bf16[272,1280]{1,0:T(8,128)(2,1)} %other_part.5), channel_id=1, source_target_pairs={{4,0},{8,12},{5,1},{9,13},{6,2},{10,14},{7,3},{11,15},{20,16},{24,... | collective-permute-start | bytes 2088968 | tf_op jit(solution)/shard_map/ppermute | solution.py:602
  113.8 24.2 %collective-permute-start.7 = (bf16[272,1280]{1,0:T(8,128)(2,1)}, bf16[272,1280]{1,0:T(8,128)(2,1)}, u32[]{:S(2)}, u32[]{:S(2)}) collective-permute-start(bf16[272,1280]{1,0:T(8,128)(2,1)} %other_part.4), channel_id=1, source_target_pairs={{0,4},{12,8},{1,5},{13,9},{2,6},{14,10},{3,7},{15,11},{16,20},{28,... | collective-permute-start | bytes 2088968 | tf_op jit(solution)/shard_map/ppermute | solution.py:602
  128.1 26.1 %collective-permute-start.10 = (bf16[272,1280]{1,0:T(8,128)(2,1)}, bf16[272,1280]{1,0:T(8,128)(2,1)}, u32[]{:S(2)}, u32[]{:S(2)}) collective-permute-start(bf16[272,1280]{1,0:T(8,128)(2,1)} %other_part.7), channel_id=1, source_target_pairs={{4,12},{8,0},{5,13},{9,1},{6,14},{10,2},{7,15},{11,3},{20,28},{24,... | collective-permute-start | bytes 2088968 | tf_op jit(solution)/shard_map/ppermute | solution.py:602
